TPU v7x, 256 devices: a whole 4x4x8 slice. The times are simulated.
256 devices in a mesh: row: 8 (over y, core), col: 8 (over z), depth: 4 (over x).
Axes of the slice: x: 4, y: 4, z: 8, core: 2. Of those that a mesh axis runs over, the one named last changes fastest.
Arguments:
- blocks: bfloat16 [512, 13, 128, 128], P(('row', 'col'), None, 'depth'), may hold values from -1.1953125 to 1.1953125
- pattern: int32 [512, 13], replicated, may hold values from 0 to 511, as said below
- place: int32 [512], replicated, may hold values from 0 to 511, as said below
Outputs:
- square: bfloat16 [512, 13, 128, 128], P(('row', 'col'), None, 'depth')
Inputs may be any that keep to these rules, and one draw needn't show every extreme that they name: `place`: A permutation of the block rows; block j is stored in a slot s with (s // 8) mod 8 = j mod 8. `pattern`: row s lists the 13 distinct block columns of the block row b stored in slot s, in increasing order of their offset o in (b + o) mod 512, with offsets within -12 to 12, one of them 0; in every row at most 2 of the columns are equal mod 8, and some residue has exactly 2.
All inputs are finite; a program needn't handle non-finite values.
Results may differ from a plain program's by a relative error of at most 0.013.
Values may be sent and summed in bfloat16 or wider, within the bound.
A program may use at most 128 MiB of HBM per device.

v0:
```python
import jax
import jax.numpy as jnp
from jax import lax
from jax.sharding import PartitionSpec as P


def body(blocks, pattern, place):
    n_col = lax.axis_size("col")
    n_depth = lax.axis_size("depth")
    my_row = lax.axis_index("row")
    my_col = lax.axis_index("col")
    rows_dev, entries, quarter, block_width = blocks.shape
    capacity = (entries + n_col - 1) // n_col
    group_size = rows_dev * n_col
    column_panel = lax.all_gather(blocks, "row", axis=0, tiled=True)

    def chosen_slots(row_cols):
        slot_ids = place[row_cols]
        owner_col = slot_ids // rows_dev % n_col
        onehot = owner_col[..., None] == jnp.arange(n_col, dtype=jnp.int32)
        rank_in = jnp.cumsum(onehot.astype(jnp.int32), axis=1) - 1
        return onehot[..., None] & (rank_in[..., None] == jnp.arange(capacity, dtype=jnp.int32))

    panel_rows = lax.all_gather(blocks, "col", axis=0, tiled=True)
    row_count = panel_rows.shape[0]
    slot_ids = my_row * group_size + jnp.arange(row_count, dtype=jnp.int32)
    row_cols = pattern[slot_ids]
    picked = lax.dynamic_index_in_dim(chosen_slots(row_cols), my_col, axis=2, keepdims=False)
    is_mine = picked.astype(jnp.int32)
    filled = jnp.sum(is_mine, axis=1)
    target_block = jnp.sum(is_mine * row_cols[:, :, None], axis=1)
    target_slot = place[target_block]
    panel_pos = target_slot // group_size * rows_dev + target_slot % rows_dev
    far_rows = column_panel[panel_pos]
    far_cols = pattern[target_slot]
    matches = (row_cols[:, None, :, None] == far_cols[:, :, None, :]) & (
        filled[:, :, None, None] > 0
    )
    aligned = jnp.einsum(
        "nmxy,nmyqs->nmxqs",
        matches.astype(jnp.bfloat16),
        far_rows,
        preferred_element_type=jnp.float32,
    ).astype(jnp.bfloat16)
    partial_value = jnp.einsum(
        "nxqr,nmxqs->nmrs", panel_rows, aligned, preferred_element_type=jnp.float32
    )
    rounded = partial_value.astype(jnp.bfloat16)
    shaped = rounded.reshape(n_col, rows_dev, capacity, n_depth, quarter, block_width)
    arrived = lax.all_to_all(
        lax.all_to_all(shaped, "col", split_axis=0, concat_axis=0, tiled=True),
        "depth",
        split_axis=3,
        concat_axis=3,
        tiled=True,
    )
    finished = jnp.sum(arrived, axis=3, dtype=jnp.float32).astype(jnp.bfloat16)
    own_slots = (my_row * n_col + my_col) * rows_dev + jnp.arange(rows_dev, dtype=jnp.int32)
    own_cols = pattern[own_slots]
    placing = chosen_slots(own_cols).astype(jnp.bfloat16)
    result = jnp.einsum("weck,cwkqs->weqs", placing, finished, preferred_element_type=jnp.float32)
    return result.astype(jnp.bfloat16)


def solution(mesh):
    placed = (P(("row", "col"), None, "depth", None), P(), P())
    return jax.shard_map(
        body,
        mesh=mesh,
        in_specs=placed,
        out_specs=P(("row", "col"), None, "depth", None),
        check_vma=False,
    )
```

profile of v0, /device:TPU:1, one launch (start us, length us, event | category | flops | bytes accessed | tf_op | source)
XLA Modules:
  0.0 321.5 jit_solution(6728229043838272940)
XLA Ops:
  6.5 0.0 copy-start
  6.5 0.0 all-gather.3.cloned.1.call-start
  6.5 0.7 all-gather.3.cloned.1.call-update
  7.3 0.0 all-gather.5.cloned.1.call-start
  7.3 0.7 all-gather.5.cloned.1.call-update
  8.0 0.9 copy.53
  8.9 0.6 gather_fusion.2
  9.5 0.1 copy.56
  9.6 0.1 reshape.293
  9.8 0.0 copy-done
  9.8 5.4 %gather_fusion.3 = s32[832]{0:T(1024)S(1)} fusion(s32[512]{0:T(512)S(1)} %copy-done, s32[1024]{0:T(1024)S(1)} %pad_clamp_fusion.3), kind=kCustom, calls=%fused_computation.3 | custom fusion | bytes 9984 | tf_op jit(solution)/shard_map/gather | solution.py:18
  15.2 0.1 reshape.292
  15.4 0.1 copy.55
  15.5 0.1 reduce_window_sum.23
  15.7 0.1 copy.57
  15.8 0.1 reshape.301
  15.9 1.3 gather_fusion.4
  17.2 0.1 gather.34
  17.3 0.1 copy.58
  17.4 0.1 copy.61
  17.5 0.1 reshape.309
  17.7 0.6 gather_fusion.5
  18.3 0.1 copy.67
  18.4 0.1 reshape.317
  18.6 0.1 copy.63
  18.7 40.4 %all-gather.3.cloned.1.call-done = bf16[64,13,32,128]{3,2,1,0:T(8,128)(2,1)} async-done(((bf16[8,13,32,128]{3,2,1,0:T(8,128)(2,1)}), bf16[64,13,32,128]{3,2,1,0:T(8,128)(2,1)}) %all-gather.3.cloned.1.call-update) | async-done | bytes 6815760 | tf_op jit(solution)/shard_map/all_gather | solution.py:15
  59.1 11.8 %gather_fusion.6 = bf16[128,13,32,128]{3,2,1,0:T(8,128)(2,1)} fusion(bf16[64,13,32,128]{3,2,1,0:T(8,128)(2,1)} %all-gather.3.cloned.1.call-done, s32[1024]{0:T(1024)S(1)} %pad_clamp_fusion), kind=kCustom, calls=%fused_computation.6 | custom fusion | bytes 27263488 | tf_op jit(solution)/shard_map/gather | solution.py:34
  70.9 14.9 %fusion.4 = bf16[64,2,13,32,128]{4,2,3,1,0:T(8,128)(2,1)} fusion(bf16[64,2,13,32,128]{4,3,2,1,0:T(8,128)(2,1)} %bitcast.54, s32[64,2,13]{2,1,0:T(2,128)S(1)} %bitcast.56, s32[64,13]{1,0:T(8,128)S(1)} %gather_fusion.2, pred[64,2]{1,0:T(8,128)(4,1)S(1)} %copy.63), kind=kOutput, calls=%fused_computation.11 | convolution fusion | flops 184068352 | bytes 27273088 | tf_op jit(solution)/shard_map/nmxy,nmyqs->nmxqs/dot_general | solution.py:39
  85.8 54.2 %all-gather.5.cloned.1.call-done = bf16[64,13,32,128]{3,2,1,0:T(8,128)(2,1)} async-done(((bf16[8,13,32,128]{3,2,1,0:T(8,128)(2,1)}), bf16[64,13,32,128]{3,2,1,0:T(8,128)(2,1)}) %all-gather.5.cloned.1.call-update) | async-done | bytes 6815760 | tf_op jit(solution)/shard_map/all_gather | solution.py:24
  140.0 13.2 %bitcast_convert_fusion = bf16[64,2,128,128]{2,3,1,0:T(8,128)(2,1)} fusion(bf16[64,13,32,128]{3,2,1,0:T(8,128)(2,1)} %all-gather.5.cloned.1.call-done, bf16[64,2,13,32,128]{4,2,3,1,0:T(8,128)(2,1)} %fusion.4), kind=kOutput, calls=%fused_computation.12 | convolution fusion | flops 1746927616 | bytes 24641536 | tf_op jit(solution)/shard_map/nxqr,nmxqs->nmrs/dot_general | solution.py:45
  153.2 3.5 %copy.70 = bf16[8,8,2,4,32,128]{5,4,2,1,3,0:T(8,128)(2,1)S(1)} copy(bf16[8,8,2,4,32,128]{5,4,3,2,1,0:T(8,128)(2,1)} %bitcast.55) | data formatting | bytes 8388608 | tf_op jit(solution)/shard_map/reshape | solution.py:49
  156.7 98.5 %all_to_all.10 = bf16[8,8,2,4,32,128]{5,4,2,1,3,0:T(8,128)(2,1)S(1)} all-to-all(bf16[8,8,2,4,32,128]{5,4,2,1,3,0:T(8,128)(2,1)S(1)} %copy.70), channel_id=1, replica_groups=mesh['row'=8,'col'=8,'depth'=4] {'col'}, dimensions={0} | all-to-all | bytes 8388608 | tf_op jit(solution)/shard_map/all_to_all | solution.py:51
  255.2 3.0 copy.71
  258.2 4.9 %all-to-all-start.1 = ((bf16[8,8,2,4,32,128]{5,4,2,1,0,3:T(8,128)(2,1)}), bf16[8,8,2,4,32,128]{5,4,2,1,0,3:T(8,128)(2,1)}, u32[]{:S(2)}, u32[]{:S(2)}) async-start(bf16[8,8,2,4,32,128]{5,4,2,1,0,3:T(8,128)(2,1)} %copy.71), calls=%async_computation.1 | async-start | bytes 8388608 | tf_op jit(solution)/shard_map/all_to_all | solution.py:50
  263.1 0.6 gather_fusion
  263.7 0.1 reshape.277
  263.8 1.3 gather_fusion.1
  265.0 0.1 reshape.276
  265.2 1.3 reduce_window_sum.22
  266.5 43.0 %all-to-all-done.1 = bf16[8,8,2,4,32,128]{5,4,2,1,0,3:T(8,128)(2,1)} async-done(((bf16[8,8,2,4,32,128]{5,4,2,1,0,3:T(8,128)(2,1)}), bf16[8,8,2,4,32,128]{5,4,2,1,0,3:T(8,128)(2,1)}, u32[]{:S(2)}, u32[]{:S(2)}) %all-to-all-start.1) | async-done | bytes 4194336 | tf_op jit(solution)/shard_map/all_to_all | solution.py:50
  309.5 3.3 %reduce_sum.35 = bf16[8,8,2,32,128]{4,3,2,1,0:T(8,128)(2,1)S(1)} reduce(bf16[8,8,2,4,32,128]{5,4,2,1,0,3:T(8,128)(2,1)} %all-to-all-done.1, bf16[]{:T(256)} %constant.109.clone.1), dimensions={3}, to_apply=%region_4.5 | reduce | flops 1572864 | bytes 5242882 | tf_op jit(solution)/shard_map/reduce_sum | solution.py:57
  312.8 0.8 bitcast_convert_fusion.1
  313.6 1.1 copy.74
  (23 shorter events, 0.3 us)
Async XLA Ops:
  6.5 3.3 %copy-start = (s32[512]{0:T(512)S(1)}, s32[512]{0:T(512)}, u32[]{:S(2)}) copy-start(s32[512]{0:T(512)} %param.5) | copy-start | bytes 6148
  6.5 52.6 %all-gather.3.cloned.1.call-start = ((), (), s32[]{:S(2)}) async-start(), calls=%async_computation.2 | async-start | bytes 7667712 | tf_op jit(solution)/shard_map/all_gather | solution.py:15
  7.3 132.8 %all-gather.5.cloned.1.call-start = ((), (), s32[]{:S(2)}) async-start(), calls=%async_computation.3 | async-start | bytes 7667712 | tf_op jit(solution)/shard_map/all_gather | solution.py:24
  258.2 51.3 %all-to-all-start.1 = ((bf16[8,8,2,4,32,128]{5,4,2,1,0,3:T(8,128)(2,1)}), bf16[8,8,2,4,32,128]{5,4,2,1,0,3:T(8,128)(2,1)}, u32[]{:S(2)}, u32[]{:S(2)}) async-start(bf16[8,8,2,4,32,128]{5,4,2,1,0,3:T(8,128)(2,1)} %copy.71), calls=%async_computation.1 | async-start | bytes 8388608 | tf_op jit(solution)/shard_map/all_to_all | solution.py:50
Sparse Core Ops, SparseCore 0:
  9.2 49.9 all-gather.2
  60.9 79.0 all-gather.4
where the time goes:
time: 324 us; the launch traced here: 322 us
  waiting for transfers between devices  139 us (43%)
  blocking collectives  98.5 us (30%)
  local copies, waits for them, and re-layouts  31.7 us (10%)
  matrix products  28.9 us (9%)
  between operations  13.7 us (4%)
  starting transfers between devices  4.9 us (2%)
  other arithmetic  4.9 us (2%)
    all_to_all x1, blocking collectives, body(): lax.all_to_all(shaped, 'col', split_axis=0, concat_axis=0, tiled=True)  98.5 us
    all_gather x1, waiting for transfers between devices, body(): panel_rows = lax.all_gather(blocks, 'col', axis=0, tiled=True)  54.2 us
    all_to_all x1, waiting for transfers between devices, body(): lax.all_to_all(lax.all_to_all(shaped, 'col', split_axis=0, concat_axis=0,...  43 us
    all_gather x1, waiting for transfers between devices, body(): column_panel = lax.all_gather(blocks, 'row', axis=0, tiled=True)  40.4 us
    dot_general x1, matrix products, body(): jnp.einsum('nmxy,nmyqs->nmxqs', matches.astype(jnp.bfloat16), far_rows, p...  14.9 us
    dot_general x1, matrix products, body(): jnp.einsum('nxqr,nmxqs->nmrs', panel_rows, aligned, preferred_element_typ...  13.2 us
    gather x1, local copies, waits for them, and re-layouts, body(): far_rows = column_panel[panel_pos]  11.8 us
    gather x4, local copies, waits for them, and re-layouts, chosen_slots(): slot_ids = place[row_cols]  6.92 us
  transfers between devices with their start and end apart: 3, of which 3 were waited for; matrix products, arithmetic and copies ran while one was open for 13% of the time, Pallas kernels for 0%

commit v1 on v0

v1 whole, which is shorter than its diff:
```python
import functools

import jax
import jax.numpy as jnp
from jax import lax
from jax.experimental import pallas as pl
from jax.experimental.pallas import tpu as pltpu
from jax.sharding import PartitionSpec as P

MESH = pl.DeviceIdType.MESH
F32 = jnp.float32
BF16 = jnp.bfloat16


def kernel(
    n_row, n_col, n_depth, rd, entries, cap,
    own_ref, meta_ref, out_ref,
    panel, lhs, part, half_in, full_in, back, pick_v, place_v, pick, place_s,
    y_send, y_recv, z_send, z_recv, h_send, h_recv, f_send, f_recv,
    b_send, b_recv, local_sem,
):
    r, c, d = lax.axis_index("row"), lax.axis_index("col"), lax.axis_index("depth")
    shard = rd * entries
    piece = shard // 2
    group = rd * n_col
    lanes = cap * group
    zero_block = n_row * shard
    blocks_unit = rd * cap

    def ring(me, step, size):
        return lax.rem(me + (step + size), size)

    def at_row(step):
        return (ring(r, step, n_row), c, d)

    def at_col(step):
        return (r, ring(c, step, n_col), d)

    def at_depth(step):
        return (r, c, ring(d, step, n_depth))

    far = n_col // 2
    barrier = pltpu.get_barrier_semaphore()
    partners = [at_row(1), at_row(-1), at_depth(1), at_depth(-1)]
    partners += [at_col(s) for s in range(1, n_col)]
    for other in partners:
        pl.semaphore_signal(barrier, inc=1, device_id=other, device_id_type=MESH)
    pl.semaphore_wait(barrier, len(partners))

    def y_copy(way, t, h):
        sign = 1 if way == 0 else -1
        owner = ring(r, -sign * (t - 1), n_row)
        span = pl.ds(owner * shard + h * piece, piece)
        src = own_ref.at[pl.ds(h * piece, piece)] if t == 1 else panel.at[span]
        return pltpu.make_async_remote_copy(
            src_ref=src, dst_ref=panel.at[span],
            send_sem=y_send.at[way, t - 1, h], recv_sem=y_recv.at[way, t - 1, h],
            device_id=at_row(sign), device_id_type=MESH,
        )

    def y_arrived(way, t, h):
        sign = 1 if way == 0 else -1
        owner = ring(r, -sign * t, n_row)
        span = pl.ds(owner * shard + h * piece, piece)
        pltpu.make_async_remote_copy(
            src_ref=panel.at[span], dst_ref=panel.at[span],
            send_sem=y_send.at[way, t - 1, h], recv_sem=y_recv.at[way, t - 1, h],
            device_id=at_row(sign), device_id_type=MESH,
        ).wait_recv()

    def z_unit(way, t):
        return 2 * t - 1 + (way if t < far else 0)

    def z_copy(way, t, h):
        sign = 1 if way == 0 else -1
        span = pl.ds(h * piece, piece)
        src = own_ref.at[span] if t == 1 else lhs.at[z_unit(way, t - 1) - 1, span]
        return pltpu.make_async_remote_copy(
            src_ref=src, dst_ref=lhs.at[z_unit(way, t) - 1, span],
            send_sem=z_send.at[way, t - 1, h], recv_sem=z_recv.at[way, t - 1, h],
            device_id=at_col(sign), device_id_type=MESH,
        )

    def used(t, way, h, size):
        return t < size // 2 or (t == size // 2 and h == way)

    def y_step(t, h):
        for way in range(2):
            if used(t, way, h, n_row):
                y_arrived(way, t, h)
                if used(t + 1, way, h, n_row):
                    y_copy(way, t + 1, h).start()

    def z_step(t, h):
        for way in range(2):
            if used(t, way, h, n_col):
                z_copy(way, t, h).wait_recv()
                if used(t + 1, way, h, n_col):
                    z_copy(way, t + 1, h).start()

    for h in range(2):
        for way in range(2):
            y_copy(way, 1, h).start()
            z_copy(way, 1, h).start()
    own_copy = pltpu.make_async_copy(
        own_ref, panel.at[pl.ds(r * shard, shard)], local_sem.at[0]
    )
    own_copy.start()
    panel[zero_block] = jnp.zeros((panel.shape[1], panel.shape[2]), BF16)

    nb = meta_ref.shape[0]
    lane_row = lax.broadcasted_iota(jnp.int32, (group, lanes), 1) % group
    pick_row = lax.broadcasted_iota(jnp.int32, (group, lanes), 0) == lane_row
    mine = meta_ref[pl.ds(pl.multiple_of(r * group, group), group), :]
    cols = [
        jnp.sum(jnp.where(pick_row, mine[:, x : x + 1], 0), axis=0, keepdims=True)
        for x in range(entries)
    ]
    lane = lax.broadcasted_iota(jnp.int32, (1, lanes), 1)
    rank = lane // group
    target = jnp.full((1, lanes), -1, jnp.int32)
    seen = jnp.zeros((1, lanes), jnp.int32)
    for x in range(entries):
        hit = lax.rem(cols[x], n_col) == c
        target = jnp.where(hit & (seen == rank), cols[x], target)
        seen = seen + hit.astype(jnp.int32)
    ids = lax.broadcasted_iota(jnp.int32, (nb, lanes), 0)
    slot = jnp.sum(
        jnp.where(ids == target, meta_ref[:, entries : entries + 1], 0), axis=0, keepdims=True
    )
    at_slot = ids == slot
    base = (slot // group * rd + lax.rem(slot, rd)) * entries
    found = [jnp.full((1, lanes), zero_block, jnp.int32) for _ in range(entries)]
    for y in range(entries):
        far_col = jnp.sum(
            jnp.where(at_slot, meta_ref[:, y : y + 1], 0), axis=0, keepdims=True
        )
        for x in range(entries):
            found[x] = jnp.where(
                (cols[x] == far_col) & (target >= 0), base + y, found[x]
            )
    for x in range(entries):
        pick_v[pl.ds(x, 1), :] = found[x]

    own_rows = meta_ref[pl.ds(pl.multiple_of((r * n_col + c) * rd, rd), rd), :]
    width = own_rows.shape[1]
    kind = lax.rem(own_rows, n_col)
    entry = lax.broadcasted_iota(jnp.int32, (rd, width), 1)
    before = jnp.zeros((rd, width), jnp.int32)
    for x in range(entries):
        before = before + ((kind == kind[:, x : x + 1]) & (entry > x)).astype(jnp.int32)
    home = kind * blocks_unit + lax.broadcasted_iota(jnp.int32, (rd, width), 0) * cap + before
    place_v[:, pl.ds(0, width)] = home
    pick_copy = pltpu.make_async_copy(pick_v, pick, local_sem.at[1])
    place_copy = pltpu.make_async_copy(place_v, place_s, local_sem.at[2])
    pick_copy.start()
    place_copy.start()

    def offset(u):
        if u == 0:
            return 0
        t = (u + 1) // 2
        return -t if u % 2 == 1 else t

    quarter = panel.shape[1]

    def multiply(u):
        source = ring(c, offset(u), n_col)

        def one_row(w, carry):
            n = source * rd + w
            if u == 0:
                left = own_ref[pl.ds(w * entries, entries)]
            else:
                left = lhs[u - 1, pl.ds(w * entries, entries)]
            left = left.reshape(entries * quarter, left.shape[2])
            right = jnp.concatenate(
                [
                    jnp.concatenate(
                        [panel[pick[x, m * group + n]] for x in range(entries)], axis=0
                    )
                    for m in range(cap)
                ],
                axis=1,
            )
            product = lax.dot_general(
                left, right, (((0,), (0,)), ((), ())), preferred_element_type=F32
            ).astype(BF16)
            width = left.shape[1]
            for q in range(n_depth):
                for m in range(cap):
                    part[u, q, w * cap + m] = product[
                        q * quarter : (q + 1) * quarter, m * width : (m + 1) * width
                    ]
            return carry

        lax.fori_loop(0, rd, one_row, 0)

    mid = blocks_unit // 2
    spans = (pl.ds(0, mid), pl.ds(mid, mid))

    def half_copy(u, way):
        return pltpu.make_async_remote_copy(
            src_ref=part.at[u, ring(d, 2, n_depth), spans[way]],
            dst_ref=half_in.at[u, way],
            send_sem=h_send.at[u, way], recv_sem=h_recv.at[u, way],
            device_id=at_depth(1 if way == 0 else -1), device_id_type=MESH,
        )

    def full_copy(u, way):
        step = 1 if way == 0 else -1
        return pltpu.make_async_remote_copy(
            src_ref=part.at[u, ring(d, step, n_depth)],
            dst_ref=full_in.at[u, way],
            send_sem=f_send.at[u, way], recv_sem=f_recv.at[u, way],
            device_id=at_depth(step), device_id_type=MESH,
        )

    def back_copy(u, home_of):
        span = pl.ds(home_of * blocks_unit, blocks_unit)
        return pltpu.make_async_remote_copy(
            src_ref=part.at[u, d], dst_ref=back.at[span],
            send_sem=b_send.at[u], recv_sem=b_recv.at[u],
            device_id=at_col(offset(u)), device_id_type=MESH,
        )

    def first(u):
        for way in range(2):
            half_copy(u, way).start()

    def second(u):
        for way in range(2):
            half_copy(u, way).wait_recv()
            q = ring(d, 1 if way == 0 else -1, n_depth)
            total = part[u, q, spans[way]].astype(F32) + half_in[u, way].astype(F32)
            part[u, q, spans[way]] = total.astype(BF16)
            full_copy(u, way).start()

    def third(u):
        for way in range(2):
            full_copy(u, way).wait_recv()
        total = part[u, d].astype(F32) + full_in[u, 0].astype(F32) + full_in[u, 1].astype(F32)
        if u == 0:
            back[pl.ds(c * blocks_unit, blocks_unit)] = total.astype(BF16)
        else:
            part[u, d] = total.astype(BF16)
            back_copy(u, c).start()

    y_step(1, 0)
    y_step(1, 1)
    z_step(1, 0)
    y_step(2, 0)
    y_step(2, 1)
    z_step(1, 1)
    y_step(3, 0)
    y_step(3, 1)
    z_step(2, 0)
    y_step(4, 0)
    y_step(4, 1)
    own_copy.wait()
    pick_copy.wait()
    place_copy.wait()

    multiply(0)
    first(0)
    multiply(1)
    first(1)
    second(0)
    z_step(2, 1)
    multiply(2)
    first(2)
    second(1)
    third(0)
    multiply(3)
    first(3)
    second(2)
    third(1)
    z_step(3, 0)
    multiply(4)
    first(4)
    second(3)
    third(2)
    z_step(3, 1)
    multiply(5)
    first(5)
    second(4)
    third(3)
    multiply(6)
    first(6)
    second(5)
    third(4)
    z_step(4, 0)
    z_step(4, 1)
    multiply(7)
    first(7)
    second(6)
    third(5)
    second(7)
    third(6)
    third(7)

    for u in range(1, n_col):
        back_copy(u, ring(c, -offset(u), n_col)).wait_recv()
    for w in range(rd):
        for a in range(entries):
            out_ref[w * entries + a] = back[place_s[w, a]]

    for way in range(2):
        for t in range(1, far + 1):
            for h in range(2):
                if used(t, way, h, n_row):
                    y_copy(way, t, h).wait_send()
                if used(t, way, h, n_col):
                    z_copy(way, t, h).wait_send()
        for u in range(n_col):
            half_copy(u, way).wait_send()
            full_copy(u, way).wait_send()
    for u in range(1, n_col):
        back_copy(u, c).wait_send()


def solution(mesh):
    n_row, n_col, n_depth = mesh.shape["row"], mesh.shape["col"], mesh.shape["depth"]

    def body(blocks, pattern, place):
        rd, entries, quarter, width = blocks.shape
        cap = (entries + n_col - 1) // n_col
        shard, unit = rd * entries, rd * cap
        lanes = cap * rd * n_col
        meta = jnp.concatenate([pattern, place[:, None]], axis=1)
        dma, vmem = pltpu.SemaphoreType.DMA, pltpu.VMEM
        result = pl.pallas_call(
            functools.partial(kernel, n_row, n_col, n_depth, rd, entries, cap),
            out_shape=jax.ShapeDtypeStruct((shard, quarter, width), BF16),
            in_specs=[pl.BlockSpec(memory_space=pltpu.VMEM)] * 2,
            out_specs=pl.BlockSpec(memory_space=pltpu.VMEM),
            scratch_shapes=[
                vmem((n_row * shard + 1, quarter, width), BF16),
                vmem((n_col - 1, shard, quarter, width), BF16),
                vmem((n_col, n_depth, unit, quarter, width), BF16),
                vmem((n_col, 2, unit // 2, quarter, width), BF16),
                vmem((n_col, 2, unit, quarter, width), BF16),
                vmem((n_col * unit, quarter, width), BF16),
                vmem((16, lanes), jnp.int32),
                vmem((8, 128), jnp.int32),
                pltpu.SMEM((16, lanes), jnp.int32),
                pltpu.SMEM((8, 128), jnp.int32),
                dma((2, n_row // 2, 2)), dma((2, n_row // 2, 2)),
                dma((2, n_col // 2, 2)), dma((2, n_col // 2, 2)),
                dma((n_col, 2)), dma((n_col, 2)),
                dma((n_col, 2)), dma((n_col, 2)),
                dma((n_col,)), dma((n_col,)),
                dma((3,)),
            ],
            compiler_params=pltpu.CompilerParams(
                collective_id=0, has_side_effects=True, vmem_limit_bytes=48 * 2**20
            ),
        )(blocks.reshape(shard, quarter, width), meta)
        return result.reshape(blocks.shape)

    placed = (P(("row", "col"), None, "depth", None), P(), P())
    return jax.shard_map(
        body,
        mesh=mesh,
        in_specs=placed,
        out_specs=P(("row", "col"), None, "depth", None),
        check_vma=False,
    )
```

time: 324 us -> 103 us (0.32)
  the two profiles are of different devices: /device:TPU:1 before, /device:TPU:8 now
where the time goes in v1:
time: 103 us
  Pallas kernels  99.6 us (97%)
  local copies, waits for them, and re-layouts  2.88 us (3%)
    pallas_call x1, Pallas kernels, body(): pl.pallas_call(functools.partial(kernel, n_row, n_col, n_depth, rd, entri...  99.6 us
    unnamed x5, local copies, waits for them, and re-layouts  2.74 us

profile of v1, /device:TPU:8, one launch (start us, length us, event | category | flops | bytes accessed | tf_op | source)
XLA Modules:
  0.0 103.2 jit_solution(68168759029359500)
XLA Ops:
  0.0 0.0 copy-start.1
  0.0 0.7 copy-done.1
  0.7 0.8 pad_add_fusion
  1.4 0.1 copy.7.meta_ref
  1.6 0.0 copy-start
  1.6 1.2 %copy-done = bf16[8,13,32,128]{3,2,1,0:T(8,128)(2,1)S(1)} copy-done((bf16[8,13,32,128]{3,2,1,0:T(8,128)(2,1)S(1)}, bf16[8,13,32,128]{3,2,1,0:T(8,128)(2,1)}, u32[]{:S(2)}) %copy-start) | copy-done | bytes 851992
  2.8 99.6 %shard_map.37 = bf16[104,32,128]{2,1,0:T(8,128)(2,1)S(1)} custom-call(bf16[104,32,128]{2,1,0:T(8,128)(2,1)S(1)} %bitcast.4, s32[512,14]{1,0:T(8,128)S(1)} %copy.7.meta_ref), custom_call_target="tpu_custom_call" | custom-call | tf_op jit(solution)/shard_map/pallas_call | solution.py:332
  102.3 0.9 copy.9
Async XLA Ops:
  0.0 0.7 copy-start.1
  1.6 1.2 %copy-start = (bf16[8,13,32,128]{3,2,1,0:T(8,128)(2,1)S(1)}, bf16[8,13,32,128]{3,2,1,0:T(8,128)(2,1)}, u32[]{:S(2)}) copy-start(bf16[8,13,32,128]{3,2,1,0:T(8,128)(2,1)} %param.3) | copy-start | bytes 2555908

commit v2 on v1

v2 whole, which is shorter than its diff:
```python
import functools

import jax
import jax.numpy as jnp
from jax import lax
from jax.experimental import pallas as pl
from jax.experimental.pallas import tpu as pltpu
from jax.sharding import PartitionSpec as P

MESH = pl.DeviceIdType.MESH
F32 = jnp.float32
BF16 = jnp.bfloat16
REACH = 3
PIECES = 4


def kernel(
    n_row, n_col, n_depth, rd, entries, cap,
    own_ref, pattern_ref, place_ref, out_ref,
    panel, panel2, lhs, part, half_in, full_in, back,
    pattern_v, place_v, meta, pick_v, home_v, pick, home,
    y_send, y_recv, y4_send, y4_recv, z_send, z_recv,
    v_send, v_recv, v4_send, v4_recv,
    h_send, h_recv, f_send, f_recv, b_send, b_recv, local_sem,
):
    r, c, d = lax.axis_index("row"), lax.axis_index("col"), lax.axis_index("depth")
    core, odd = lax.rem(r, 2), lax.rem(c, 2)
    shard = rd * entries
    piece = shard // PIECES
    half = shard // 2
    group = rd * n_col
    lanes = cap * group
    zero_block = n_row * shard
    unit = rd * cap
    far = n_col // 2

    def ring(me, step, size):
        return lax.rem(me + step + size, size)

    def at_row(step):
        return (ring(r, step, n_row), c, d)

    def at_col(step):
        return (r, ring(c, step, n_col), d)

    def at_depth(step):
        return (r, c, ring(d, step, n_depth))

    def remote(src, dst, send, recv, to):
        return pltpu.make_async_remote_copy(
            src_ref=src, dst_ref=dst, send_sem=send, recv_sem=recv,
            device_id=to, device_id_type=MESH,
        )

    partners = [at_row(1), at_row(-1), at_depth(1), at_depth(-1)]
    partners += [at_col(s) for s in range(-REACH, REACH + 1) if s != 0]
    pattern_copy = pltpu.make_async_copy(pattern_ref, pattern_v, local_sem.at[3])
    place_copy = pltpu.make_async_copy(place_ref, place_v, local_sem.at[4])
    own_copy = pltpu.make_async_copy(
        own_ref, panel.at[pl.ds(r * shard, shard)], local_sem.at[0]
    )
    pattern_copy.start()
    place_copy.start()
    own_copy.start()
    barrier = pltpu.get_barrier_semaphore()
    for other in partners:
        pl.semaphore_signal(barrier, inc=1, device_id=other, device_id_type=MESH)
    pl.semaphore_wait(barrier, len(partners))

    signs = (1, -1)
    side = 1 - 2 * core

    def span_of(owner, p, size):
        return pl.ds(owner * shard + p * size, size)

    def y_copy(way, t, h, owner_step):
        span = span_of(ring(r, owner_step, n_row), h, half)
        src = own_ref.at[pl.ds(h * half, half)] if t == 1 else panel.at[span]
        return remote(
            src, panel.at[span], y_send.at[way, t - 1, h], y_recv.at[way, t - 1, h],
            at_row(signs[way]),
        )

    def y_out(way, t, h):
        return y_copy(way, t, h, -signs[way] * (t - 1))

    def y_in(way, t, h):
        span = span_of(ring(r, -signs[way] * t, n_row), h, half)
        remote(
            panel.at[span], panel.at[span], y_send.at[way, t - 1, h],
            y_recv.at[way, t - 1, h], at_row(signs[way]),
        ).wait_recv()

    def y4_copy(h, owner):
        span = span_of(owner, h, half)
        return remote(
            panel.at[span], panel.at[span], y4_send.at[h], y4_recv.at[h], at_row(side)
        )

    def y4_out(h):
        return y4_copy(h, ring(r, -3 * side, n_row))

    def y_step(t, h):
        for way in range(2):
            y_in(way, t, h)
            if t < 3:
                y_out(way, t + 1, h).start()
        if t == 3:
            y4_out(h).start()

    mate = 1 - odd

    def v_out(way, t, p):
        span = span_of(ring(r, -signs[way] * (t - 1), n_row), p, piece)
        src = lhs.at[mate, pl.ds(p * piece, piece)] if t == 1 else panel2.at[span]
        return remote(
            src, panel2.at[span], v_send.at[way, t - 1, p], v_recv.at[way, t - 1, p],
            at_row(signs[way]),
        )

    def v_in(way, t, p):
        span = span_of(ring(r, -signs[way] * t, n_row), p, piece)
        remote(
            panel2.at[span], panel2.at[span], v_send.at[way, t - 1, p],
            v_recv.at[way, t - 1, p], at_row(signs[way]),
        ).wait_recv()

    def v4_copy(p, owner):
        span = span_of(owner, p, piece)
        return remote(
            panel2.at[span], panel2.at[span], v4_send.at[p], v4_recv.at[p], at_row(side)
        )

    def v4_out(p):
        return v4_copy(p, ring(r, -3 * side, n_row))

    def v_first(p):
        for way in range(2):
            v_out(way, 1, p).start()

    def v_step(t, p):
        for way in range(2):
            v_in(way, t, p)
            if t < 3:
                v_out(way, t + 1, p).start()
        if t == 3:
            v4_out(p).start()

    def z_copy(way, t, p):
        span = pl.ds(p * piece, piece)
        src = own_ref.at[span] if t == 1 else lhs.at[2 * t - 4 + way, span]
        return remote(
            src, lhs.at[2 * t - 2 + way, span],
            z_send.at[way, t - 1, p], z_recv.at[way, t - 1, p], at_col(signs[way]),
        )

    def z_first(p):
        for way in range(2):
            z_copy(way, 1, p).start()

    def z_step(t, p):
        for way in range(2):
            z_copy(way, t, p).wait_recv()
            if t < REACH:
                z_copy(way, t + 1, p).start()

    for h in range(2):
        for way in range(2):
            y_out(way, 1, h).start()
        z_first(h)
    panel[zero_block] = jnp.zeros((panel.shape[1], panel.shape[2]), BF16)
    panel2[zero_block] = jnp.zeros((panel.shape[1], panel.shape[2]), BF16)

    nb = meta.shape[0]
    pattern_copy.wait()
    place_copy.wait()
    pad = jnp.zeros((128 - entries - 1, nb), jnp.int32)
    meta[...] = jnp.transpose(
        jnp.concatenate([pattern_v[...], place_v[...], pad], axis=0)
    )[:, : meta.shape[1]]
    partner = c + 1 - 2 * odd
    opposite = ring(c, far, n_col)
    visitor = ring(partner, far, n_col)
    lane_of = lax.broadcasted_iota(jnp.int32, (group, lanes), 1) % group
    lane_row = jnp.where(lane_of // rd == opposite, lane_of + (visitor - opposite) * rd, lane_of)
    pick_row = lax.broadcasted_iota(jnp.int32, (group, lanes), 0) == lane_row
    mine = meta[pl.ds(pl.multiple_of(r * group, group), group), :]
    cols = [
        jnp.sum(jnp.where(pick_row, mine[:, x : x + 1], 0), axis=0, keepdims=True)
        for x in range(entries)
    ]
    lane = lax.broadcasted_iota(jnp.int32, (1, lanes), 1)
    rank = lane // group
    wanted = jnp.where((lane % group) // rd == opposite, partner, c)
    target = jnp.full((1, lanes), -1, jnp.int32)
    seen = jnp.zeros((1, lanes), jnp.int32)
    for x in range(entries):
        hit = lax.rem(cols[x], n_col) == wanted
        target = jnp.where(hit & (seen == rank), cols[x], target)
        seen = seen + hit.astype(jnp.int32)
    ids = lax.broadcasted_iota(jnp.int32, (nb, lanes), 0)
    slot = jnp.sum(
        jnp.where(ids == target, meta[:, entries : entries + 1], 0), axis=0, keepdims=True
    )
    at_slot = ids == slot
    base = (slot // group * rd + lax.rem(slot, rd)) * entries
    found = [jnp.full((1, lanes), zero_block, jnp.int32) for _ in range(entries)]
    for y in range(entries):
        far_col = jnp.sum(
            jnp.where(at_slot, meta[:, y : y + 1], 0), axis=0, keepdims=True
        )
        for x in range(entries):
            found[x] = jnp.where(
                (cols[x] == far_col) & (target >= 0), base + y, found[x]
            )
    for x in range(entries):
        pick_v[pl.ds(x, 1), :] = found[x]

    own_rows = meta[pl.ds(pl.multiple_of((r * n_col + c) * rd, rd), rd), :]
    width = own_rows.shape[1]
    kind = lax.rem(own_rows, n_col)
    entry = lax.broadcasted_iota(jnp.int32, (rd, width), 1)
    before = jnp.zeros((rd, width), jnp.int32)
    for x in range(entries):
        before = before + ((kind == kind[:, x : x + 1]) & (entry > x)).astype(jnp.int32)
    spot = kind * unit + lax.broadcasted_iota(jnp.int32, (rd, width), 0) * cap + before
    home_v[:, pl.ds(0, width)] = spot
    pick_copy = pltpu.make_async_copy(pick_v, pick, local_sem.at[1])
    home_copy = pltpu.make_async_copy(home_v, home, local_sem.at[2])
    pick_copy.start()
    home_copy.start()

    def offset(u):
        t = (u + 1) // 2
        return 0 if u == 0 else (far if t == far else (-t if u % 2 == 1 else t))

    quarter = panel.shape[1]
    rows_h = rd // 2
    blocks_h = unit // 2

    def multiply(u, h):
        source = ring(c, offset(u), n_col)
        table = panel if u < n_col - 1 else panel2

        def one_row(w, carry):
            n = source * rd + w
            if u == 0:
                left = panel[pl.ds(r * shard + w * entries, entries)]
            elif u < n_col - 1:
                left = lhs[u - 1, pl.ds(w * entries, entries)]
            else:
                left = lhs[2 * REACH - 2 + odd, pl.ds(w * entries, entries)]
            left = left.reshape(entries * quarter, left.shape[2])
            right = jnp.concatenate(
                [
                    jnp.concatenate(
                        [table[pick[x, m * group + n]] for x in range(entries)], axis=0
                    )
                    for m in range(cap)
                ],
                axis=1,
            )
            product = lax.dot_general(
                left, right, (((0,), (0,)), ((), ())), preferred_element_type=F32
            ).astype(BF16)
            width = left.shape[1]
            for q in range(n_depth):
                for m in range(cap):
                    part[u, q, w * cap + m] = product[
                        q * quarter : (q + 1) * quarter, m * width : (m + 1) * width
                    ]
            return carry

        lax.fori_loop(h * rows_h, (h + 1) * rows_h, one_row, 0)

    mid = blocks_h // 2

    def mids(h, way):
        return pl.ds(h * blocks_h + way * mid, mid)

    def half_copy(u, h, way):
        return remote(
            part.at[u, ring(d, 2, n_depth), mids(h, way)], half_in.at[u, mids(h, way)],
            h_send.at[u, h, way], h_recv.at[u, h, way], at_depth(signs[way]),
        )

    def full_copy(u, h, way):
        span = pl.ds(h * blocks_h, blocks_h)
        return remote(
            part.at[u, ring(d, signs[way], n_depth), span], full_in.at[u, way, span],
            f_send.at[u, h, way], f_recv.at[u, h, way], at_depth(signs[way]),
        )

    def shift(u):
        return 2 * REACH * odd - REACH if u == n_col - 1 else offset(u)

    def back_copy(u, h, kind_of):
        span = pl.ds(kind_of * unit + h * blocks_h, blocks_h)
        return remote(
            part.at[u, d, pl.ds(h * blocks_h, blocks_h)], back.at[span],
            b_send.at[u, h], b_recv.at[u, h], at_col(shift(u)),
        )

    def back_out(u, h):
        return back_copy(u, h, partner if u == n_col - 1 else c)

    def first(u, h):
        for way in range(2):
            half_copy(u, h, way).start()

    def second(u, h):
        for way in range(2):
            half_copy(u, h, way).wait_recv()
            q = ring(d, signs[way], n_depth)
            total = part[u, q, mids(h, way)].astype(F32) + half_in[u, mids(h, way)].astype(F32)
            part[u, q, mids(h, way)] = total.astype(BF16)
            full_copy(u, h, way).start()

    def third(u, h):
        for way in range(2):
            full_copy(u, h, way).wait_recv()
        span = pl.ds(h * blocks_h, blocks_h)
        total = (
            part[u, d, span].astype(F32)
            + full_in[u, 0, span].astype(F32)
            + full_in[u, 1, span].astype(F32)
        ).astype(BF16)
        if u == 0:
            back[pl.ds(c * unit + h * blocks_h, blocks_h)] = total
        else:
            part[u, d, span] = total

    items = [(0, 0), (0, 1)] + [(u, 0) for u in range(1, 7)]
    items += [(u, 1) for u in range(1, 7)] + [(7, 0), (7, 1)]
    done = {"mul": 0, "second": 0, "third": 0, "back": 0}

    def work(n=1):
        for _ in range(n):
            k = done["mul"]
            if k < len(items):
                multiply(*items[k])
                first(*items[k])
                done["mul"] = k + 1

    def add(n=1):
        for _ in range(n):
            k = done["second"]
            if k < done["mul"]:
                second(*items[k])
                done["second"] = k + 1

    def finish(n=1):
        for _ in range(n):
            k = done["third"]
            if k < done["second"]:
                third(*items[k])
                done["third"] = k + 1

    def give():
        while done["back"] < done["third"]:
            item = items[done["back"]]
            if item[0] > 0:
                back_out(*item).start()
            done["back"] += 1

    y_step(1, 0)
    z_step(1, 0)
    y_step(1, 1)
    z_step(1, 1)
    y_step(2, 0)
    z_step(2, 0)
    y_step(2, 1)
    z_step(2, 1)
    y_step(3, 0)
    z_step(3, 0)
    z_first(2)
    z_first(3)
    v_first(0)
    v_first(1)
    y_step(3, 1)
    z_step(3, 1)
    own_copy.wait()
    pick_copy.wait()
    home_copy.wait()
    for h in range(2):
        y4_copy(h, ring(r, 4, n_row)).wait_recv()

    work()
    v_step(1, 0)
    work(2)
    add()
    z_step(1, 2)
    v_step(1, 1)
    work()
    add()
    work()
    v_step(2, 0)
    finish()
    add()
    work()
    add()
    z_step(1, 3)
    pltpu.make_async_copy(
        lhs.at[mate], panel2.at[pl.ds(r * shard, shard)], local_sem.at[5]
    ).start()
    v_step(2, 1)
    finish()
    work()
    add()
    work()
    finish()
    v_step(3, 0)
    v_first(2)
    v_first(3)
    work()
    add()
    finish()
    z_step(2, 2)
    v_step(3, 1)
    work()
    add()
    finish()
    v_step(1, 2)
    add()
    finish()
    z_step(2, 3)
    v_step(1, 3)
    work()
    add()
    finish()
    work()
    v_step(2, 2)
    add()
    finish()
    z_step(3, 2)
    v_step(2, 3)
    add()
    finish()
    v_step(3, 2)
    add()
    finish()
    z_step(3, 3)
    finish()
    give()
    work()
    add()
    finish()
    work()
    v_step(3, 3)
    pltpu.make_async_copy(
        lhs.at[mate], panel2.at[pl.ds(r * shard, shard)], local_sem.at[5]
    ).wait()
    for p in range(PIECES):
        v4_copy(p, ring(r, 4, n_row)).wait_recv()
    work()
    add()
    finish()
    give()
    work()
    for _ in range(len(items)):
        add()
        finish()
        give()

    for u in range(1, n_col):
        for h in range(2):
            kind_of = ring(c, -offset(u), n_col)
            back_copy(u, h, kind_of).wait_recv()
    for w in range(rd):
        for a in range(entries):
            out_ref[w * entries + a] = back[home[w, a]]

    for way in range(2):
        for t in range(1, REACH + 1):
            for h in range(2):
                y_out(way, t, h).wait_send()
            for p in range(PIECES):
                z_copy(way, t, p).wait_send()
                v_out(way, t, p).wait_send()
        for u in range(n_col):
            for h in range(2):
                half_copy(u, h, way).wait_send()
                full_copy(u, h, way).wait_send()
    for h in range(2):
        y4_out(h).wait_send()
        for u in range(1, n_col):
            back_out(u, h).wait_send()
    for p in range(PIECES):
        v4_out(p).wait_send()


def solution(mesh):
    n_row, n_col, n_depth = mesh.shape["row"], mesh.shape["col"], mesh.shape["depth"]

    def body(blocks, pattern, place):
        rd, entries, quarter, width = blocks.shape
        nb = pattern.shape[0]
        cap = (entries + n_col - 1) // n_col
        shard, unit = rd * entries, rd * cap
        lanes = cap * rd * n_col
        dma, vmem, ints = pltpu.SemaphoreType.DMA, pltpu.VMEM, jnp.int32
        result = pl.pallas_call(
            functools.partial(kernel, n_row, n_col, n_depth, rd, entries, cap),
            out_shape=jax.ShapeDtypeStruct((shard, quarter, width), BF16),
            in_specs=[pl.BlockSpec(memory_space=pl.ANY)] * 3,
            out_specs=pl.BlockSpec(memory_space=pltpu.VMEM),
            scratch_shapes=[
                vmem((n_row * shard + 1, quarter, width), BF16),
                vmem((n_row * shard + 1, quarter, width), BF16),
                vmem((2 * REACH, shard, quarter, width), BF16),
                vmem((n_col, n_depth, unit, quarter, width), BF16),
                vmem((n_col, unit, quarter, width), BF16),
                vmem((n_col, 2, unit, quarter, width), BF16),
                vmem((n_col * unit, quarter, width), BF16),
                vmem((entries, nb), ints), vmem((1, nb), ints), vmem((nb, 16), ints),
                vmem((16, lanes), ints), vmem((8, 128), ints),
                pltpu.SMEM((16, lanes), ints), pltpu.SMEM((8, 128), ints),
                dma((2, 3, 2)), dma((2, 3, 2)), dma((2,)), dma((2,)),
                dma((2, REACH, PIECES)), dma((2, REACH, PIECES)),
                dma((2, 3, PIECES)), dma((2, 3, PIECES)), dma((PIECES,)), dma((PIECES,)),
                dma((n_col, 2, 2)), dma((n_col, 2, 2)),
                dma((n_col, 2, 2)), dma((n_col, 2, 2)),
                dma((n_col, 2)), dma((n_col, 2)),
                dma((6,)),
            ],
            compiler_params=pltpu.CompilerParams(
                collective_id=0, has_side_effects=True, vmem_limit_bytes=62 * 2**20
            ),
        )(blocks.reshape(shard, quarter, width), pattern.T, place.reshape(1, nb))
        return result.reshape(blocks.shape)

    placed = (P(("row", "col"), None, "depth", None), P(), P())
    return jax.shard_map(
        body,
        mesh=mesh,
        in_specs=placed,
        out_specs=P(("row", "col"), None, "depth", None),
        check_vma=False,
    )
```

time: 103 us -> 100 us (0.971)
  the two profiles are of different devices: /device:TPU:8 before, /device:TPU:1 now
where the time goes in v2:
time: 100 us; the launch traced here: 98.7 us
  Pallas kernels  96.6 us (97%)
  local copies, waits for them, and re-layouts  2.11 us (2%)
    pallas_call x1, Pallas kernels, body(): pl.pallas_call(functools.partial(kernel, n_row, n_col, n_depth, rd, entri...  96.6 us
    unnamed x1, local copies, waits for them, and re-layouts  2.11 us

profile of v2, /device:TPU:1, one launch (start us, length us, event | category | flops | bytes accessed | tf_op | source)
XLA Modules:
  0.0 98.7 jit_solution(14281086577289094565)
XLA Ops:
  0.0 96.6 %shard_map.37 = bf16[104,32,128]{2,1,0:T(8,128)(2,1)} custom-call(bf16[104,32,128]{2,1,0:T(8,128)(2,1)} %bitcast.5, s32[13,512]{1,0:T(8,128)} %bitcast.6, s32[1,512]{1,0:T(1,128)} %bitcast.7), custom_call_target="tpu_custom_call" | custom-call | tf_op jit(solution)/shard_map/pallas_call | solution.py:502
  96.6 2.1 %copy.5 = bf16[8,13,32,128]{3,2,1,0:T(8,128)(2,1)} copy(bf16[8,13,32,128]{3,2,1,0:T(8,128)(2,1)} %bitcast.4) | data formatting | bytes 1703936

commit v3 on v2

--- a/solution.py
+++ b/solution.py
@@ -12,6 +12,26 @@
 BF16 = jnp.bfloat16
 REACH = 3
 PIECES = 4
+
+ORDER = (
+    ("idx",), ("y", 1, 0), ("z", 1, 0), ("y", 1, 1), ("z", 1, 1), ("y", 2, 0), ("z", 2, 0),
+    ("zf", 2), ("y", 2, 1), ("z", 2, 1), ("zf", 3), ("y", 3, 0), ("z", 3, 0), ("vf", 0),
+    ("vf", 1), ("y", 3, 1), ("z", 1, 2), ("panel",), ("mul", 3, 0), ("v", 1, 0), ("mul", 4, 0),
+    ("v", 1, 1), ("z", 3, 1), ("mul", 5, 0), ("add", 3, 0), ("mul", 6, 0), ("add", 4, 0),
+    ("v", 2, 0), ("mul", 1, 0), ("z", 1, 3), ("v", 2, 1), ("add", 5, 0), ("add", 6, 0),
+    ("end", 3, 0), ("mul", 2, 0), ("v", 3, 0), ("vf", 2), ("vf", 3), ("z", 2, 2),
+    ("add", 1, 0), ("end", 5, 0), ("end", 4, 0), ("v", 3, 1), ("mul", 1, 1), ("add", 2, 0),
+    ("end", 6, 0), ("mul", 2, 1), ("z", 2, 3), ("v", 1, 2), ("give", 5, 0), ("add", 1, 1),
+    ("v", 1, 3), ("give", 6, 0), ("give", 3, 0), ("give", 4, 0), ("end", 1, 0), ("give", 1, 0),
+    ("end", 2, 0), ("add", 2, 1), ("give", 2, 0), ("mul", 3, 1), ("z", 3, 2), ("mul", 4, 1),
+    ("v", 2, 2), ("end", 1, 1), ("give", 1, 1), ("mul", 0, 0), ("v", 2, 3), ("add", 3, 1),
+    ("z", 3, 3), ("add", 4, 1), ("end", 2, 1), ("give", 2, 1), ("mul", 5, 1), ("v", 3, 2),
+    ("add", 0, 0), ("mul", 6, 1), ("v", 3, 3), ("end", 3, 1), ("give", 3, 1), ("end", 4, 1),
+    ("give", 4, 1), ("add", 5, 1), ("panel2",), ("mul", 7, 0), ("mul", 7, 1), ("add", 6, 1),
+    ("end", 0, 0), ("end", 5, 1), ("give", 5, 1), ("mul", 0, 1), ("add", 7, 0), ("add", 7, 1),
+    ("end", 6, 1), ("give", 6, 1), ("add", 0, 1), ("end", 7, 0), ("give", 7, 0), ("end", 7, 1),
+    ("give", 7, 1), ("end", 0, 1),
+)
 
 
 def kernel(
@@ -330,137 +350,43 @@
         else:
             part[u, d, span] = total
 
-    items = [(0, 0), (0, 1)] + [(u, 0) for u in range(1, 7)]
-    items += [(u, 1) for u in range(1, 7)] + [(7, 0), (7, 1)]
-    done = {"mul": 0, "second": 0, "third": 0, "back": 0}
-
-    def work(n=1):
-        for _ in range(n):
-            k = done["mul"]
-            if k < len(items):
-                multiply(*items[k])
-                first(*items[k])
-                done["mul"] = k + 1
-
-    def add(n=1):
-        for _ in range(n):
-            k = done["second"]
-            if k < done["mul"]:
-                second(*items[k])
-                done["second"] = k + 1
-
-    def finish(n=1):
-        for _ in range(n):
-            k = done["third"]
-            if k < done["second"]:
-                third(*items[k])
-                done["third"] = k + 1
-
-    def give():
-        while done["back"] < done["third"]:
-            item = items[done["back"]]
-            if item[0] > 0:
-                back_out(*item).start()
-            done["back"] += 1
-
-    y_step(1, 0)
-    z_step(1, 0)
-    y_step(1, 1)
-    z_step(1, 1)
-    y_step(2, 0)
-    z_step(2, 0)
-    y_step(2, 1)
-    z_step(2, 1)
-    y_step(3, 0)
-    z_step(3, 0)
-    z_first(2)
-    z_first(3)
-    v_first(0)
-    v_first(1)
-    y_step(3, 1)
-    z_step(3, 1)
-    own_copy.wait()
-    pick_copy.wait()
-    home_copy.wait()
-    for h in range(2):
-        y4_copy(h, ring(r, 4, n_row)).wait_recv()
-
-    work()
-    v_step(1, 0)
-    work(2)
-    add()
-    z_step(1, 2)
-    v_step(1, 1)
-    work()
-    add()
-    work()
-    v_step(2, 0)
-    finish()
-    add()
-    work()
-    add()
-    z_step(1, 3)
-    pltpu.make_async_copy(
+    mate_copy = pltpu.make_async_copy(
         lhs.at[mate], panel2.at[pl.ds(r * shard, shard)], local_sem.at[5]
-    ).start()
-    v_step(2, 1)
-    finish()
-    work()
-    add()
-    work()
-    finish()
-    v_step(3, 0)
-    v_first(2)
-    v_first(3)
-    work()
-    add()
-    finish()
-    z_step(2, 2)
-    v_step(3, 1)
-    work()
-    add()
-    finish()
-    v_step(1, 2)
-    add()
-    finish()
-    z_step(2, 3)
-    v_step(1, 3)
-    work()
-    add()
-    finish()
-    work()
-    v_step(2, 2)
-    add()
-    finish()
-    z_step(3, 2)
-    v_step(2, 3)
-    add()
-    finish()
-    v_step(3, 2)
-    add()
-    finish()
-    z_step(3, 3)
-    finish()
-    give()
-    work()
-    add()
-    finish()
-    work()
-    v_step(3, 3)
-    pltpu.make_async_copy(
-        lhs.at[mate], panel2.at[pl.ds(r * shard, shard)], local_sem.at[5]
-    ).wait()
-    for p in range(PIECES):
-        v4_copy(p, ring(r, 4, n_row)).wait_recv()
-    work()
-    add()
-    finish()
-    give()
-    work()
-    for _ in range(len(items)):
-        add()
-        finish()
-        give()
+    )
+    here = []
+
+    def z_event(t, p):
+        z_step(t, p)
+        if t == 1:
+            here.append(p)
+            if len(here) == PIECES:
+                mate_copy.start()
+
+    def whole_panel():
+        own_copy.wait()
+        pick_copy.wait()
+        home_copy.wait()
+        for h in range(2):
+            y4_copy(h, ring(r, 4, n_row)).wait_recv()
+
+    def whole_panel2():
+        mate_copy.wait()
+        for p in range(PIECES):
+            v4_copy(p, ring(r, 4, n_row)).wait_recv()
+
+    def mul(u, h):
+        multiply(u, h)
+        first(u, h)
+
+    steps = {
+        "y": y_step, "z": z_event, "zf": z_first, "v": v_step, "vf": v_first,
+        "panel": whole_panel, "panel2": whole_panel2,
+        "mul": mul, "add": second, "end": third,
+        "give": lambda u, h: back_out(u, h).start(),
+    }
+    for step in ORDER:
+        if step[0] != "idx":
+            steps[step[0]](*step[1:])
 
     for u in range(1, n_col):
         for h in range(2):
@@ -502,7 +428,7 @@
         result = pl.pallas_call(
             functools.partial(kernel, n_row, n_col, n_depth, rd, entries, cap),
             out_shape=jax.ShapeDtypeStruct((shard, quarter, width), BF16),
-            in_specs=[pl.BlockSpec(memory_space=pl.ANY)] * 3,
+            in_specs=[pl.BlockSpec(memory_space=pltpu.HBM)] * 3,
             out_specs=pl.BlockSpec(memory_space=pltpu.VMEM),
             scratch_shapes=[
                 vmem((n_row * shard + 1, quarter, width), BF16),

time: 100 us -> 97.3 us (0.973); the launches traced: 98.7 us -> 97.1 us
  Pallas kernels: 96.6 us -> 95 us
    pallas_call x1, Pallas kernels: 96.6 us -> 95 us  [body(): pl.pallas_call(functools.partial(kernel, n_row, n_col, n_depth, rd, entri...]
where the time goes in v3:
time: 97.3 us; the launch traced here: 97.1 us
  Pallas kernels  95 us (98%)
  local copies, waits for them, and re-layouts  2.11 us (2%)
    pallas_call x1, Pallas kernels, body(): pl.pallas_call(functools.partial(kernel, n_row, n_col, n_depth, rd, entri...  95 us
    unnamed x1, local copies, waits for them, and re-layouts  2.11 us

profile of v3, /device:TPU:1, one launch (start us, length us, event | category | flops | bytes accessed | tf_op | source)
XLA Modules:
  0.0 97.1 jit_solution(7571538093345958731)
XLA Ops:
  0.0 95.0 %shard_map.37 = bf16[104,32,128]{2,1,0:T(8,128)(2,1)} custom-call(bf16[104,32,128]{2,1,0:T(8,128)(2,1)} %bitcast.5, s32[13,512]{1,0:T(8,128)} %bitcast.6, s32[1,512]{1,0:T(1,128)} %bitcast.7), custom_call_target="tpu_custom_call" | custom-call | tf_op jit(solution)/shard_map/pallas_call | solution.py:428
  95.0 2.1 %copy.5 = bf16[8,13,32,128]{3,2,1,0:T(8,128)(2,1)} copy(bf16[8,13,32,128]{3,2,1,0:T(8,128)(2,1)} %bitcast.4) | data formatting | bytes 1703936

commit v4 on v3

--- a/solution.py
+++ b/solution.py
@@ -14,22 +14,23 @@
 PIECES = 4
 
 ORDER = (
-    ("idx",), ("y", 1, 0), ("z", 1, 0), ("y", 1, 1), ("z", 1, 1), ("y", 2, 0), ("z", 2, 0),
-    ("zf", 2), ("y", 2, 1), ("z", 2, 1), ("zf", 3), ("y", 3, 0), ("z", 3, 0), ("vf", 0),
-    ("vf", 1), ("y", 3, 1), ("z", 1, 2), ("panel",), ("mul", 3, 0), ("v", 1, 0), ("mul", 4, 0),
-    ("v", 1, 1), ("z", 3, 1), ("mul", 5, 0), ("add", 3, 0), ("mul", 6, 0), ("add", 4, 0),
-    ("v", 2, 0), ("mul", 1, 0), ("z", 1, 3), ("v", 2, 1), ("add", 5, 0), ("add", 6, 0),
-    ("end", 3, 0), ("mul", 2, 0), ("v", 3, 0), ("vf", 2), ("vf", 3), ("z", 2, 2),
-    ("add", 1, 0), ("end", 5, 0), ("end", 4, 0), ("v", 3, 1), ("mul", 1, 1), ("add", 2, 0),
-    ("end", 6, 0), ("mul", 2, 1), ("z", 2, 3), ("v", 1, 2), ("give", 5, 0), ("add", 1, 1),
-    ("v", 1, 3), ("give", 6, 0), ("give", 3, 0), ("give", 4, 0), ("end", 1, 0), ("give", 1, 0),
-    ("end", 2, 0), ("add", 2, 1), ("give", 2, 0), ("mul", 3, 1), ("z", 3, 2), ("mul", 4, 1),
-    ("v", 2, 2), ("end", 1, 1), ("give", 1, 1), ("mul", 0, 0), ("v", 2, 3), ("add", 3, 1),
-    ("z", 3, 3), ("add", 4, 1), ("end", 2, 1), ("give", 2, 1), ("mul", 5, 1), ("v", 3, 2),
-    ("add", 0, 0), ("mul", 6, 1), ("v", 3, 3), ("end", 3, 1), ("give", 3, 1), ("end", 4, 1),
-    ("give", 4, 1), ("add", 5, 1), ("panel2",), ("mul", 7, 0), ("mul", 7, 1), ("add", 6, 1),
-    ("end", 0, 0), ("end", 5, 1), ("give", 5, 1), ("mul", 0, 1), ("add", 7, 0), ("add", 7, 1),
-    ("end", 6, 1), ("give", 6, 1), ("add", 0, 1), ("end", 7, 0), ("give", 7, 0), ("end", 7, 1),
+    ("index", 0), ("index", 1), ("index", 2), ("index", 3), ("y", 1, 0), ("z", 1, 0),
+    ("y", 1, 1), ("z", 1, 1), ("y", 2, 0), ("z", 2, 0), ("zf", 2), ("y", 2, 1), ("z", 2, 1),
+    ("zf", 3), ("y", 3, 0), ("z", 3, 0), ("vf", 0), ("vf", 1), ("y", 3, 1), ("z", 1, 2),
+    ("panel",), ("mul", 3, 0), ("v", 1, 0), ("mul", 4, 0), ("v", 1, 1), ("z", 3, 1),
+    ("mul", 5, 0), ("add", 3, 0), ("mul", 6, 0), ("add", 4, 0), ("v", 2, 0), ("mul", 1, 0),
+    ("z", 1, 3), ("v", 2, 1), ("add", 5, 0), ("add", 6, 0), ("end", 3, 0), ("mul", 2, 0),
+    ("v", 3, 0), ("vf", 2), ("vf", 3), ("z", 2, 2), ("add", 1, 0), ("end", 5, 0),
+    ("end", 4, 0), ("v", 3, 1), ("mul", 1, 1), ("add", 2, 0), ("end", 6, 0), ("mul", 2, 1),
+    ("z", 2, 3), ("v", 1, 2), ("give", 5, 0), ("add", 1, 1), ("v", 1, 3), ("give", 6, 0),
+    ("give", 3, 0), ("give", 4, 0), ("end", 1, 0), ("give", 1, 0), ("end", 2, 0),
+    ("add", 2, 1), ("give", 2, 0), ("mul", 3, 1), ("z", 3, 2), ("mul", 4, 1), ("v", 2, 2),
+    ("end", 1, 1), ("give", 1, 1), ("mul", 0, 0), ("v", 2, 3), ("add", 3, 1), ("z", 3, 3),
+    ("add", 4, 1), ("end", 2, 1), ("give", 2, 1), ("mul", 5, 1), ("v", 3, 2), ("add", 0, 0),
+    ("mul", 6, 1), ("v", 3, 3), ("end", 3, 1), ("give", 3, 1), ("end", 4, 1), ("give", 4, 1),
+    ("add", 5, 1), ("panel2",), ("mul", 7, 0), ("mul", 7, 1), ("add", 6, 1), ("end", 0, 0),
+    ("end", 5, 1), ("give", 5, 1), ("mul", 0, 1), ("add", 7, 0), ("add", 7, 1), ("end", 6, 1),
+    ("give", 6, 1), ("add", 0, 1), ("end", 7, 0), ("give", 7, 0), ("end", 7, 1),
     ("give", 7, 1), ("end", 0, 1),
 )
 
@@ -73,7 +74,7 @@
         )
 
     partners = [at_row(1), at_row(-1), at_depth(1), at_depth(-1)]
-    partners += [at_col(s) for s in range(-REACH, REACH + 1) if s != 0]
+    partners += [at_col(1), at_col(-1)]
     pattern_copy = pltpu.make_async_copy(pattern_ref, pattern_v, local_sem.at[3])
     place_copy = pltpu.make_async_copy(place_ref, place_v, local_sem.at[4])
     own_copy = pltpu.make_async_copy(
@@ -192,63 +193,80 @@
     panel2[zero_block] = jnp.zeros((panel.shape[1], panel.shape[2]), BF16)
 
     nb = meta.shape[0]
-    pattern_copy.wait()
-    place_copy.wait()
-    pad = jnp.zeros((128 - entries - 1, nb), jnp.int32)
-    meta[...] = jnp.transpose(
-        jnp.concatenate([pattern_v[...], place_v[...], pad], axis=0)
-    )[:, : meta.shape[1]]
     partner = c + 1 - 2 * odd
     opposite = ring(c, far, n_col)
     visitor = ring(partner, far, n_col)
-    lane_of = lax.broadcasted_iota(jnp.int32, (group, lanes), 1) % group
-    lane_row = jnp.where(lane_of // rd == opposite, lane_of + (visitor - opposite) * rd, lane_of)
-    pick_row = lax.broadcasted_iota(jnp.int32, (group, lanes), 0) == lane_row
-    mine = meta[pl.ds(pl.multiple_of(r * group, group), group), :]
-    cols = [
-        jnp.sum(jnp.where(pick_row, mine[:, x : x + 1], 0), axis=0, keepdims=True)
-        for x in range(entries)
-    ]
-    lane = lax.broadcasted_iota(jnp.int32, (1, lanes), 1)
-    rank = lane // group
-    wanted = jnp.where((lane % group) // rd == opposite, partner, c)
-    target = jnp.full((1, lanes), -1, jnp.int32)
-    seen = jnp.zeros((1, lanes), jnp.int32)
-    for x in range(entries):
-        hit = lax.rem(cols[x], n_col) == wanted
-        target = jnp.where(hit & (seen == rank), cols[x], target)
-        seen = seen + hit.astype(jnp.int32)
-    ids = lax.broadcasted_iota(jnp.int32, (nb, lanes), 0)
-    slot = jnp.sum(
-        jnp.where(ids == target, meta[:, entries : entries + 1], 0), axis=0, keepdims=True
-    )
-    at_slot = ids == slot
-    base = (slot // group * rd + lax.rem(slot, rd)) * entries
-    found = [jnp.full((1, lanes), zero_block, jnp.int32) for _ in range(entries)]
-    for y in range(entries):
-        far_col = jnp.sum(
-            jnp.where(at_slot, meta[:, y : y + 1], 0), axis=0, keepdims=True
-        )
-        for x in range(entries):
-            found[x] = jnp.where(
-                (cols[x] == far_col) & (target >= 0), base + y, found[x]
-            )
-    for x in range(entries):
-        pick_v[pl.ds(x, 1), :] = found[x]
-
-    own_rows = meta[pl.ds(pl.multiple_of((r * n_col + c) * rd, rd), rd), :]
-    width = own_rows.shape[1]
-    kind = lax.rem(own_rows, n_col)
-    entry = lax.broadcasted_iota(jnp.int32, (rd, width), 1)
-    before = jnp.zeros((rd, width), jnp.int32)
-    for x in range(entries):
-        before = before + ((kind == kind[:, x : x + 1]) & (entry > x)).astype(jnp.int32)
-    spot = kind * unit + lax.broadcasted_iota(jnp.int32, (rd, width), 0) * cap + before
-    home_v[:, pl.ds(0, width)] = spot
     pick_copy = pltpu.make_async_copy(pick_v, pick, local_sem.at[1])
     home_copy = pltpu.make_async_copy(home_v, home, local_sem.at[2])
-    pick_copy.start()
-    home_copy.start()
+    table = {}
+
+    def index_targets():
+        pattern_copy.wait()
+        place_copy.wait()
+        pad = jnp.zeros((128 - entries - 1, nb), jnp.int32)
+        meta[...] = jnp.transpose(
+            jnp.concatenate([pattern_v[...], place_v[...], pad], axis=0)
+        )[:, : meta.shape[1]]
+        lane_of = lax.broadcasted_iota(jnp.int32, (group, lanes), 1) % group
+        lane_row = jnp.where(
+            lane_of // rd == opposite, lane_of + (visitor - opposite) * rd, lane_of
+        )
+        pick_row = lax.broadcasted_iota(jnp.int32, (group, lanes), 0) == lane_row
+        mine = meta[pl.ds(pl.multiple_of(r * group, group), group), :]
+        cols = [
+            jnp.sum(jnp.where(pick_row, mine[:, x : x + 1], 0), axis=0, keepdims=True)
+            for x in range(entries)
+        ]
+        lane = lax.broadcasted_iota(jnp.int32, (1, lanes), 1)
+        rank = lane // group
+        wanted = jnp.where((lane % group) // rd == opposite, partner, c)
+        target = jnp.full((1, lanes), -1, jnp.int32)
+        seen = jnp.zeros((1, lanes), jnp.int32)
+        for x in range(entries):
+            hit = lax.rem(cols[x], n_col) == wanted
+            target = jnp.where(hit & (seen == rank), cols[x], target)
+            seen = seen + hit.astype(jnp.int32)
+        ids = lax.broadcasted_iota(jnp.int32, (nb, lanes), 0)
+        table["slot"] = jnp.sum(
+            jnp.where(ids == target, meta[:, entries : entries + 1], 0), axis=0, keepdims=True
+        )
+        table["cols"], table["target"] = cols, target
+        table["found"] = [jnp.full((1, lanes), zero_block, jnp.int32) for _ in cols]
+
+    def index_matches(low, high):
+        slot, cols, target = table["slot"], table["cols"], table["target"]
+        at_slot = lax.broadcasted_iota(jnp.int32, (nb, lanes), 0) == slot
+        base = (slot // group * rd + lax.rem(slot, rd)) * entries
+        for y in range(low, high):
+            far_col = jnp.sum(
+                jnp.where(at_slot, meta[:, y : y + 1], 0), axis=0, keepdims=True
+            )
+            table["found"] = [
+                jnp.where((cols[x] == far_col) & (target >= 0), base + y, table["found"][x])
+                for x in range(entries)
+            ]
+
+    def index_home():
+        for x in range(entries):
+            pick_v[pl.ds(x, 1), :] = table["found"][x]
+        own_rows = meta[pl.ds(pl.multiple_of((r * n_col + c) * rd, rd), rd), :]
+        width = own_rows.shape[1]
+        kind = lax.rem(own_rows, n_col)
+        entry = lax.broadcasted_iota(jnp.int32, (rd, width), 1)
+        before = jnp.zeros((rd, width), jnp.int32)
+        for x in range(entries):
+            before = before + ((kind == kind[:, x : x + 1]) & (entry > x)).astype(jnp.int32)
+        row = lax.broadcasted_iota(jnp.int32, (rd, width), 0)
+        home_v[:, pl.ds(0, width)] = kind * unit + row * cap + before
+        pick_copy.start()
+        home_copy.start()
+
+    index_steps = (
+        index_targets,
+        lambda: index_matches(0, entries // 2),
+        lambda: index_matches(entries // 2, entries),
+        index_home,
+    )
 
     def offset(u):
         t = (u + 1) // 2
@@ -260,7 +278,7 @@
 
     def multiply(u, h):
         source = ring(c, offset(u), n_col)
-        table = panel if u < n_col - 1 else panel2
+        source_panel = panel if u < n_col - 1 else panel2
 
         def one_row(w, carry):
             n = source * rd + w
@@ -274,7 +292,7 @@
             right = jnp.concatenate(
                 [
                     jnp.concatenate(
-                        [table[pick[x, m * group + n]] for x in range(entries)], axis=0
+                        [source_panel[pick[x, m * group + n]] for x in range(entries)], axis=0
                     )
                     for m in range(cap)
                 ],
@@ -380,21 +398,12 @@
 
     steps = {
         "y": y_step, "z": z_event, "zf": z_first, "v": v_step, "vf": v_first,
-        "panel": whole_panel, "panel2": whole_panel2,
+        "index": lambda k: index_steps[k](), "panel": whole_panel, "panel2": whole_panel2,
         "mul": mul, "add": second, "end": third,
         "give": lambda u, h: back_out(u, h).start(),
     }
     for step in ORDER:
-        if step[0] != "idx":
-            steps[step[0]](*step[1:])
-
-    for u in range(1, n_col):
-        for h in range(2):
-            kind_of = ring(c, -offset(u), n_col)
-            back_copy(u, h, kind_of).wait_recv()
-    for w in range(rd):
-        for a in range(entries):
-            out_ref[w * entries + a] = back[home[w, a]]
+        steps[step[0]](*step[1:])
 
     for way in range(2):
         for t in range(1, REACH + 1):
@@ -413,6 +422,14 @@
             back_out(u, h).wait_send()
     for p in range(PIECES):
         v4_out(p).wait_send()
+
+    for u in range(1, n_col):
+        for h in range(2):
+            kind_of = ring(c, -offset(u), n_col)
+            back_copy(u, h, kind_of).wait_recv()
+    for w in range(rd):
+        for a in range(entries):
+            out_ref[w * entries + a] = back[home[w, a]]
 
 
 def solution(mesh):

time: 97.3 us -> 95 us (0.976)
  the two profiles are of different devices: /device:TPU:1 before, /device:TPU:64 now
where the time goes in v4:
time: 95 us; the launch traced here: 94.8 us
  Pallas kernels  92.7 us (98%)
  local copies, waits for them, and re-layouts  2.11 us (2%)
    pallas_call x1, Pallas kernels, body(): pl.pallas_call(functools.partial(kernel, n_row, n_col, n_depth, rd, entri...  92.7 us
    unnamed x1, local copies, waits for them, and re-layouts  2.11 us

profile of v4, /device:TPU:64, one launch (start us, length us, event | category | flops | bytes accessed | tf_op | source)
XLA Modules:
  0.0 94.8 jit_solution(8349719639385034306)
XLA Ops:
  0.0 92.7 %shard_map.37 = bf16[104,32,128]{2,1,0:T(8,128)(2,1)} custom-call(bf16[104,32,128]{2,1,0:T(8,128)(2,1)} %bitcast.5, s32[13,512]{1,0:T(8,128)} %bitcast.6, s32[1,512]{1,0:T(1,128)} %bitcast.7), custom_call_target="tpu_custom_call" | custom-call | tf_op jit(solution)/shard_map/pallas_call | solution.py:445
  92.7 2.1 %copy.5 = bf16[8,13,32,128]{3,2,1,0:T(8,128)(2,1)} copy(bf16[8,13,32,128]{3,2,1,0:T(8,128)(2,1)} %bitcast.4) | data formatting | bytes 1703936

commit v5 on v4

--- a/solution.py
+++ b/solution.py
@@ -17,21 +17,21 @@
     ("index", 0), ("index", 1), ("index", 2), ("index", 3), ("y", 1, 0), ("z", 1, 0),
     ("y", 1, 1), ("z", 1, 1), ("y", 2, 0), ("z", 2, 0), ("zf", 2), ("y", 2, 1), ("z", 2, 1),
     ("zf", 3), ("y", 3, 0), ("z", 3, 0), ("vf", 0), ("vf", 1), ("y", 3, 1), ("z", 1, 2),
-    ("panel",), ("mul", 3, 0), ("v", 1, 0), ("mul", 4, 0), ("v", 1, 1), ("z", 3, 1),
-    ("mul", 5, 0), ("add", 3, 0), ("mul", 6, 0), ("add", 4, 0), ("v", 2, 0), ("mul", 1, 0),
-    ("z", 1, 3), ("v", 2, 1), ("add", 5, 0), ("add", 6, 0), ("end", 3, 0), ("mul", 2, 0),
-    ("v", 3, 0), ("vf", 2), ("vf", 3), ("z", 2, 2), ("add", 1, 0), ("end", 5, 0),
-    ("end", 4, 0), ("v", 3, 1), ("mul", 1, 1), ("add", 2, 0), ("end", 6, 0), ("mul", 2, 1),
-    ("z", 2, 3), ("v", 1, 2), ("give", 5, 0), ("add", 1, 1), ("v", 1, 3), ("give", 6, 0),
-    ("give", 3, 0), ("give", 4, 0), ("end", 1, 0), ("give", 1, 0), ("end", 2, 0),
-    ("add", 2, 1), ("give", 2, 0), ("mul", 3, 1), ("z", 3, 2), ("mul", 4, 1), ("v", 2, 2),
-    ("end", 1, 1), ("give", 1, 1), ("mul", 0, 0), ("v", 2, 3), ("add", 3, 1), ("z", 3, 3),
-    ("add", 4, 1), ("end", 2, 1), ("give", 2, 1), ("mul", 5, 1), ("v", 3, 2), ("add", 0, 0),
-    ("mul", 6, 1), ("v", 3, 3), ("end", 3, 1), ("give", 3, 1), ("end", 4, 1), ("give", 4, 1),
-    ("add", 5, 1), ("panel2",), ("mul", 7, 0), ("mul", 7, 1), ("add", 6, 1), ("end", 0, 0),
-    ("end", 5, 1), ("give", 5, 1), ("mul", 0, 1), ("add", 7, 0), ("add", 7, 1), ("end", 6, 1),
-    ("give", 6, 1), ("add", 0, 1), ("end", 7, 0), ("give", 7, 0), ("end", 7, 1),
-    ("give", 7, 1), ("end", 0, 1),
+    ("panel",), ("mul", 1, 0), ("v", 1, 0), ("mul", 2, 0), ("mul", 3, 0), ("mul", 4, 0),
+    ("mul", 0, 0), ("mul", 0, 1), ("z", 3, 1), ("v", 1, 1), ("add", 1, 0), ("mul", 5, 0),
+    ("add", 2, 0), ("add", 3, 0), ("v", 2, 0), ("add", 4, 0), ("add", 0, 0), ("add", 0, 1),
+    ("z", 1, 3), ("v", 2, 1), ("end", 1, 0), ("mul", 6, 0), ("add", 5, 0), ("mul", 1, 1),
+    ("mul", 2, 1), ("v", 3, 0), ("vf", 2), ("vf", 3), ("end", 2, 0), ("end", 3, 0),
+    ("z", 2, 2), ("v", 3, 1), ("end", 4, 0), ("end", 0, 0), ("v", 1, 2), ("end", 0, 1),
+    ("z", 2, 3), ("add", 6, 0), ("give", 1, 0), ("give", 2, 0), ("give", 3, 0), ("give", 4, 0),
+    ("mul", 3, 1), ("v", 1, 3), ("end", 5, 0), ("add", 1, 1), ("add", 2, 1), ("give", 5, 0),
+    ("mul", 4, 1), ("v", 2, 2), ("end", 6, 0), ("z", 3, 2), ("give", 6, 0), ("add", 3, 1),
+    ("v", 2, 3), ("end", 1, 1), ("give", 1, 1), ("end", 2, 1), ("give", 2, 1), ("add", 4, 1),
+    ("v", 3, 2), ("z", 3, 3), ("mul", 5, 1), ("mul", 6, 1), ("end", 3, 1), ("give", 3, 1),
+    ("v", 3, 3), ("end", 4, 1), ("give", 4, 1), ("panel2",), ("mul", 7, 0), ("mul", 7, 1),
+    ("add", 5, 1), ("add", 6, 1), ("add", 7, 0), ("add", 7, 1), ("end", 5, 1), ("give", 5, 1),
+    ("end", 6, 1), ("give", 6, 1), ("end", 7, 0), ("give", 7, 0), ("end", 7, 1),
+    ("give", 7, 1),
 )
 
 
@@ -309,7 +309,7 @@
                     ]
             return carry
 
-        lax.fori_loop(h * rows_h, (h + 1) * rows_h, one_row, 0)
+        lax.fori_loop(h * rows_h, (h + 1) * rows_h, one_row, 0, unroll=True)
 
     mid = blocks_h // 2
 

time: 95 us -> 92.7 us (0.976)
  the two profiles are of different devices: /device:TPU:64 before, /device:TPU:57 now
where the time goes in v5:
time: 92.7 us; the launch traced here: 92.6 us
  Pallas kernels  90.5 us (98%)
  local copies, waits for them, and re-layouts  2.11 us (2%)
    pallas_call x1, Pallas kernels, body(): pl.pallas_call(functools.partial(kernel, n_row, n_col, n_depth, rd, entri...  90.5 us
    unnamed x1, local copies, waits for them, and re-layouts  2.11 us

profile of v5, /device:TPU:57, one launch (start us, length us, event | category | flops | bytes accessed | tf_op | source)
XLA Modules:
  0.0 92.6 jit_solution(1098314702882039291)
XLA Ops:
  0.0 90.5 %shard_map.37 = bf16[104,32,128]{2,1,0:T(8,128)(2,1)} custom-call(bf16[104,32,128]{2,1,0:T(8,128)(2,1)} %bitcast.5, s32[13,512]{1,0:T(8,128)} %bitcast.6, s32[1,512]{1,0:T(1,128)} %bitcast.7), custom_call_target="tpu_custom_call" | custom-call | tf_op jit(solution)/shard_map/pallas_call | solution.py:445
  90.5 2.1 %copy.5 = bf16[8,13,32,128]{3,2,1,0:T(8,128)(2,1)} copy(bf16[8,13,32,128]{3,2,1,0:T(8,128)(2,1)} %bitcast.4) | data formatting | bytes 1703936

commit v6 on v5

--- a/solution.py
+++ b/solution.py
@@ -467,9 +467,12 @@
                 dma((6,)),
             ],
             compiler_params=pltpu.CompilerParams(
-                collective_id=0, has_side_effects=True, vmem_limit_bytes=62 * 2**20
+                collective_id=0, has_side_effects=True, vmem_limit_bytes=48 * 2**20
             ),
-        )(blocks.reshape(shard, quarter, width), pattern.T, place.reshape(1, nb))
+        )(*(
+            pltpu.with_memory_space_constraint(x, pltpu.HBM)
+            for x in (blocks.reshape(shard, quarter, width), pattern.T, place.reshape(1, nb))
+        ))
         return result.reshape(blocks.shape)
 
     placed = (P(("row", "col"), None, "depth", None), P(), P())

time: 92.7 us -> 90.6 us (0.977)
  local copies, waits for them, and re-layouts: 2.11 us -> 0.9 us
    unnamed x1, local copies, waits for them, and re-layouts: 2.11 us -> 0.9 us
where the time goes in v6:
time: 90.6 us; the launch traced here: 90.5 us
  Pallas kernels  89.6 us (99%)
    pallas_call x1, Pallas kernels, body(): pl.pallas_call(functools.partial(kernel, n_row, n_col, n_depth, rd, entri...  89.6 us

profile of v6, /device:TPU:57, one launch (start us, length us, event | category | flops | bytes accessed | tf_op | source)
XLA Modules:
  0.0 90.5 jit_solution(11764353783165987997)
XLA Ops:
  0.0 89.6 %shard_map.37 = bf16[104,32,128]{2,1,0:T(8,128)(2,1)S(1)} custom-call(bf16[104,32,128]{2,1,0:T(8,128)(2,1)} %bitcast.5, s32[13,512]{1,0:T(8,128)} %bitcast.6, s32[1,512]{1,0:T(1,128)} %bitcast.7), custom_call_target="tpu_custom_call" | custom-call | tf_op jit(solution)/shard_map/pallas_call | solution.py:445
  89.6 0.9 copy.5

commit v7 on v6

--- a/solution.py
+++ b/solution.py
@@ -15,23 +15,22 @@
 
 ORDER = (
     ("index", 0), ("index", 1), ("index", 2), ("index", 3), ("y", 1, 0), ("z", 1, 0),
-    ("y", 1, 1), ("z", 1, 1), ("y", 2, 0), ("z", 2, 0), ("zf", 2), ("y", 2, 1), ("z", 2, 1),
-    ("zf", 3), ("y", 3, 0), ("z", 3, 0), ("vf", 0), ("vf", 1), ("y", 3, 1), ("z", 1, 2),
-    ("panel",), ("mul", 1, 0), ("v", 1, 0), ("mul", 2, 0), ("mul", 3, 0), ("mul", 4, 0),
-    ("mul", 0, 0), ("mul", 0, 1), ("z", 3, 1), ("v", 1, 1), ("add", 1, 0), ("mul", 5, 0),
-    ("add", 2, 0), ("add", 3, 0), ("v", 2, 0), ("add", 4, 0), ("add", 0, 0), ("add", 0, 1),
-    ("z", 1, 3), ("v", 2, 1), ("end", 1, 0), ("mul", 6, 0), ("add", 5, 0), ("mul", 1, 1),
-    ("mul", 2, 1), ("v", 3, 0), ("vf", 2), ("vf", 3), ("end", 2, 0), ("end", 3, 0),
-    ("z", 2, 2), ("v", 3, 1), ("end", 4, 0), ("end", 0, 0), ("v", 1, 2), ("end", 0, 1),
-    ("z", 2, 3), ("add", 6, 0), ("give", 1, 0), ("give", 2, 0), ("give", 3, 0), ("give", 4, 0),
-    ("mul", 3, 1), ("v", 1, 3), ("end", 5, 0), ("add", 1, 1), ("add", 2, 1), ("give", 5, 0),
-    ("mul", 4, 1), ("v", 2, 2), ("end", 6, 0), ("z", 3, 2), ("give", 6, 0), ("add", 3, 1),
-    ("v", 2, 3), ("end", 1, 1), ("give", 1, 1), ("end", 2, 1), ("give", 2, 1), ("add", 4, 1),
-    ("v", 3, 2), ("z", 3, 3), ("mul", 5, 1), ("mul", 6, 1), ("end", 3, 1), ("give", 3, 1),
-    ("v", 3, 3), ("end", 4, 1), ("give", 4, 1), ("panel2",), ("mul", 7, 0), ("mul", 7, 1),
-    ("add", 5, 1), ("add", 6, 1), ("add", 7, 0), ("add", 7, 1), ("end", 5, 1), ("give", 5, 1),
-    ("end", 6, 1), ("give", 6, 1), ("end", 7, 0), ("give", 7, 0), ("end", 7, 1),
-    ("give", 7, 1),
+    ("y", 1, 1), ("z", 1, 1), ("y", 2, 0), ("z", 1, 2), ("y", 2, 1), ("z", 1, 3), ("y", 3, 0),
+    ("z", 2, 0), ("vf", 0), ("y", 3, 1), ("z", 2, 1), ("vf", 1), ("panel",), ("mul", 1, 0),
+    ("v", 1, 0), ("mul", 2, 0), ("mul", 3, 0), ("mul", 4, 0), ("mul", 1, 1), ("mul", 2, 1),
+    ("z", 2, 2), ("v", 1, 1), ("add", 1, 0), ("add", 2, 0), ("mul", 0, 0), ("add", 3, 0),
+    ("v", 2, 0), ("add", 4, 0), ("add", 1, 1), ("add", 2, 1), ("z", 2, 3), ("v", 2, 1),
+    ("end", 1, 0), ("give", 1, 0), ("mul", 3, 1), ("mul", 4, 1), ("end", 2, 0), ("give", 2, 0),
+    ("add", 0, 0), ("v", 3, 0), ("vf", 2), ("vf", 3), ("mul", 0, 1), ("z", 3, 0),
+    ("end", 3, 0), ("give", 3, 0), ("v", 3, 1), ("end", 4, 0), ("give", 4, 0), ("end", 1, 1),
+    ("give", 1, 1), ("end", 2, 1), ("v", 1, 2), ("z", 3, 1), ("add", 3, 1), ("add", 4, 1),
+    ("give", 2, 1), ("mul", 5, 0), ("v", 1, 3), ("end", 0, 0), ("mul", 6, 0), ("add", 0, 1),
+    ("end", 3, 1), ("z", 3, 2), ("v", 2, 2), ("give", 3, 1), ("end", 4, 1), ("give", 4, 1),
+    ("add", 5, 0), ("v", 2, 3), ("add", 6, 0), ("end", 0, 1), ("z", 3, 3), ("mul", 5, 1),
+    ("v", 3, 2), ("mul", 6, 1), ("end", 5, 0), ("give", 5, 0), ("end", 6, 0), ("v", 3, 3),
+    ("give", 6, 0), ("add", 5, 1), ("add", 6, 1), ("panel2",), ("mul", 7, 0), ("mul", 7, 1),
+    ("end", 5, 1), ("give", 5, 1), ("end", 6, 1), ("give", 6, 1), ("add", 7, 0), ("add", 7, 1),
+    ("end", 7, 0), ("give", 7, 0), ("end", 7, 1), ("give", 7, 1),
 )
 
 
@@ -45,7 +44,7 @@
     h_send, h_recv, f_send, f_recv, b_send, b_recv, local_sem,
 ):
     r, c, d = lax.axis_index("row"), lax.axis_index("col"), lax.axis_index("depth")
-    core, odd = lax.rem(r, 2), lax.rem(c, 2)
+    core, odd = lax.rem(r, 2), lax.rem(c + 2, 4) // 2
     shard = rd * entries
     piece = shard // PIECES
     half = shard // 2
@@ -80,9 +79,6 @@
     own_copy = pltpu.make_async_copy(
         own_ref, panel.at[pl.ds(r * shard, shard)], local_sem.at[0]
     )
-    pattern_copy.start()
-    place_copy.start()
-    own_copy.start()
     barrier = pltpu.get_barrier_semaphore()
     for other in partners:
         pl.semaphore_signal(barrier, inc=1, device_id=other, device_id_type=MESH)
@@ -129,7 +125,7 @@
         if t == 3:
             y4_out(h).start()
 
-    mate = 1 - odd
+    mate = 3 - odd
 
     def v_out(way, t, p):
         span = span_of(ring(r, -signs[way] * (t - 1), n_row), p, piece)
@@ -186,14 +182,19 @@
                 z_copy(way, t + 1, p).start()
 
     for h in range(2):
+        z_first(h)
         for way in range(2):
             y_out(way, 1, h).start()
-        z_first(h)
+    z_first(2)
+    z_first(3)
+    pattern_copy.start()
+    place_copy.start()
+    own_copy.start()
     panel[zero_block] = jnp.zeros((panel.shape[1], panel.shape[2]), BF16)
     panel2[zero_block] = jnp.zeros((panel.shape[1], panel.shape[2]), BF16)
 
     nb = meta.shape[0]
-    partner = c + 1 - 2 * odd
+    partner = ring(c, 2 - 4 * odd, n_col)
     opposite = ring(c, far, n_col)
     visitor = ring(partner, far, n_col)
     pick_copy = pltpu.make_async_copy(pick_v, pick, local_sem.at[1])
@@ -287,7 +288,7 @@
             elif u < n_col - 1:
                 left = lhs[u - 1, pl.ds(w * entries, entries)]
             else:
-                left = lhs[2 * REACH - 2 + odd, pl.ds(w * entries, entries)]
+                left = lhs[2 + odd, pl.ds(w * entries, entries)]
             left = left.reshape(entries * quarter, left.shape[2])
             right = jnp.concatenate(
                 [
@@ -330,7 +331,7 @@
         )
 
     def shift(u):
-        return 2 * REACH * odd - REACH if u == n_col - 1 else offset(u)
+        return 4 * odd - 2 if u == n_col - 1 else offset(u)
 
     def back_copy(u, h, kind_of):
         span = pl.ds(kind_of * unit + h * blocks_h, blocks_h)
@@ -375,7 +376,7 @@
 
     def z_event(t, p):
         z_step(t, p)
-        if t == 1:
+        if t == 2:
             here.append(p)
             if len(here) == PIECES:
                 mate_copy.start()

time: 90.6 us -> 89.4 us (0.987)
  the two profiles are of different devices: /device:TPU:57 before, /device:TPU:1 now
where the time goes in v7:
time: 89.4 us; the launch traced here: 89.3 us
  Pallas kernels  88.4 us (99%)
  local copies, waits for them, and re-layouts  0.9 us (1%)
    pallas_call x1, Pallas kernels, body(): pl.pallas_call(functools.partial(kernel, n_row, n_col, n_depth, rd, entri...  88.4 us

profile of v7, /device:TPU:1, one launch (start us, length us, event | category | flops | bytes accessed | tf_op | source)
XLA Modules:
  0.0 89.3 jit_solution(15787608778269444909)
XLA Ops:
  0.0 88.4 %shard_map.37 = bf16[104,32,128]{2,1,0:T(8,128)(2,1)S(1)} custom-call(bf16[104,32,128]{2,1,0:T(8,128)(2,1)} %bitcast.5, s32[13,512]{1,0:T(8,128)} %bitcast.6, s32[1,512]{1,0:T(1,128)} %bitcast.7), custom_call_target="tpu_custom_call" | custom-call | tf_op jit(solution)/shard_map/pallas_call | solution.py:446
  88.4 0.9 %copy.5 = bf16[8,13,32,128]{3,2,1,0:T(8,128)(2,1)} copy(bf16[8,13,32,128]{3,2,1,0:T(8,128)(2,1)S(1)} %bitcast.4) | data formatting | bytes 1703936

commit v8 on v7

--- a/solution.py
+++ b/solution.py
@@ -37,7 +37,7 @@
 def kernel(
     n_row, n_col, n_depth, rd, entries, cap,
     own_ref, pattern_ref, place_ref, out_ref,
-    panel, panel2, lhs, part, half_in, full_in, back,
+    panel, panel2, lhs, part, half_in, full_in, back0, back1,
     pattern_v, place_v, meta, pick_v, home_v, pick, home,
     y_send, y_recv, y4_send, y4_recv, z_send, z_recv,
     v_send, v_recv, v4_send, v4_recv,
@@ -258,7 +258,7 @@
         for x in range(entries):
             before = before + ((kind == kind[:, x : x + 1]) & (entry > x)).astype(jnp.int32)
         row = lax.broadcasted_iota(jnp.int32, (rd, width), 0)
-        home_v[:, pl.ds(0, width)] = kind * unit + row * cap + before
+        home_v[:, pl.ds(0, width)] = kind * (unit // 2) + lax.rem(row, rd // 2) * cap + before
         pick_copy.start()
         home_copy.start()
 
@@ -273,6 +273,7 @@
         t = (u + 1) // 2
         return 0 if u == 0 else (far if t == far else (-t if u % 2 == 1 else t))
 
+    backs = (back0, back1)
     quarter = panel.shape[1]
     rows_h = rd // 2
     blocks_h = unit // 2
@@ -334,9 +335,9 @@
         return 4 * odd - 2 if u == n_col - 1 else offset(u)
 
     def back_copy(u, h, kind_of):
-        span = pl.ds(kind_of * unit + h * blocks_h, blocks_h)
-        return remote(
-            part.at[u, d, pl.ds(h * blocks_h, blocks_h)], back.at[span],
+        span = pl.ds(kind_of * blocks_h, blocks_h)
+        return remote(
+            part.at[u, d, pl.ds(h * blocks_h, blocks_h)], backs[h].at[span],
             b_send.at[u, h], b_recv.at[u, h], at_col(shift(u)),
         )
 
@@ -365,7 +366,7 @@
             + full_in[u, 1, span].astype(F32)
         ).astype(BF16)
         if u == 0:
-            back[pl.ds(c * unit + h * blocks_h, blocks_h)] = total
+            backs[h][pl.ds(c * blocks_h, blocks_h)] = total
         else:
             part[u, d, span] = total
 
@@ -424,13 +425,12 @@
     for p in range(PIECES):
         v4_out(p).wait_send()
 
-    for u in range(1, n_col):
-        for h in range(2):
-            kind_of = ring(c, -offset(u), n_col)
-            back_copy(u, h, kind_of).wait_recv()
-    for w in range(rd):
-        for a in range(entries):
-            out_ref[w * entries + a] = back[home[w, a]]
+    for h in range(2):
+        for u in range(1, n_col):
+            back_copy(u, h, ring(c, -offset(u), n_col)).wait_recv()
+        for w in range(h * rows_h, (h + 1) * rows_h):
+            for a in range(entries):
+                out_ref[w * entries + a] = backs[h][home[w, a]]
 
 
 def solution(mesh):
@@ -455,7 +455,8 @@
                 vmem((n_col, n_depth, unit, quarter, width), BF16),
                 vmem((n_col, unit, quarter, width), BF16),
                 vmem((n_col, 2, unit, quarter, width), BF16),
-                vmem((n_col * unit, quarter, width), BF16),
+                vmem((n_col * unit // 2, quarter, width), BF16),
+                vmem((n_col * unit // 2, quarter, width), BF16),
                 vmem((entries, nb), ints), vmem((1, nb), ints), vmem((nb, 16), ints),
                 vmem((16, lanes), ints), vmem((8, 128), ints),
                 pltpu.SMEM((16, lanes), ints), pltpu.SMEM((8, 128), ints),

time: 89.4 us -> 89.4 us (level)
  no operation moved by 1% of the time
where the time goes in v8:
time: 89.4 us; the launch traced here: 89.3 us
  Pallas kernels  88.4 us (99%)
  local copies, waits for them, and re-layouts  0.9 us (1%)
    pallas_call x1, Pallas kernels, body(): pl.pallas_call(functools.partial(kernel, n_row, n_col, n_depth, rd, entri...  88.4 us

profile of v8, /device:TPU:1, one launch (start us, length us, event | category | flops | bytes accessed | tf_op | source)
XLA Modules:
  0.0 89.3 jit_solution(5790518277572664020)
XLA Ops:
  0.0 88.4 %shard_map.37 = bf16[104,32,128]{2,1,0:T(8,128)(2,1)S(1)} custom-call(bf16[104,32,128]{2,1,0:T(8,128)(2,1)} %bitcast.5, s32[13,512]{1,0:T(8,128)} %bitcast.6, s32[1,512]{1,0:T(1,128)} %bitcast.7), custom_call_target="tpu_custom_call" | custom-call | tf_op jit(solution)/shard_map/pallas_call | solution.py:446
  88.4 0.9 %copy.5 = bf16[8,13,32,128]{3,2,1,0:T(8,128)(2,1)} copy(bf16[8,13,32,128]{3,2,1,0:T(8,128)(2,1)S(1)} %bitcast.4) | data formatting | bytes 1703936
